TPU v7x, 512 devices: a whole 4x8x8 slice. The times are simulated.
512 devices in a mesh: blk: 64 (over z_hi, y, core), row: 8 (over x, z_lo).
Axes of the slice: x: 4, y: 8, z: 8 (z_hi: 4, z_lo: 2; z = z_hi * 2 + z_lo), core: 2. Of those that a mesh axis runs over, the one named last changes fastest.
Arguments:
- points: float32 [16, 262144], P(None, ('blk', 'row')), may hold values from -6 to 6
- probes: float32 [16, 262144], P(None, ('blk', 'row')), may hold values from -6 to 6
- scales: float32 [16], replicated, may hold values from 0.15 to 0.6
- noise: float32 [1], replicated, may hold values from 0.1 to 1
- pairing: int32 [2], replicated, may hold values from 1 to 63, as said below
Outputs:
- product: float32 [16, 262144], P(None, ('blk', 'row'))
Inputs may be any that keep to these rules, and one draw needn't show every extreme that they name: Round r pairs block b with block b XOR pairing[r]; the 2 entries are distinct, and round 0 takes 64 - 1.
All inputs are finite; a program needn't handle non-finite values.
Results may differ from a plain program's by a relative error of at most 0.0003.
Values sent between devices are 32-bit elements; how exact they have to be, the bound alone decides.
No kernel may reach another device: no remote copies, remote signals or barrier semaphores. Data moves between devices by JAX's collectives and lax.ppermute only.
A program may use at most 64 MiB of HBM per device.

v0:
```python
import functools
import math

import jax
import jax.numpy as jnp
from jax import lax
from jax.experimental import pallas as pl
from jax.experimental.pallas import tpu as pltpu
from jax.sharding import PartitionSpec as P

f32 = jnp.float32
bf16 = jnp.bfloat16
vmem = pl.BlockSpec(memory_space=pltpu.VMEM)
smem = pl.BlockSpec(memory_space=pltpu.SMEM)
anywhere = pl.BlockSpec(memory_space=pl.ANY)

log_two = math.log(2.0)
feature_factor = math.sqrt(5.0) / log_two
shift = 1.5 / log_two
constant = 0.75 / log_two**2
probe_factor = log_two**2 / 3.0 * 2.0**shift

tile = 256
strip = 32
direct_masks = 34


def split_three(value):
    first = value.astype(bf16)
    rest = value - first.astype(f32)
    second = rest.astype(bf16)
    third = (rest - second.astype(f32)).astype(bf16)
    return first, second, third


def norm_rows(scaled, left):
    count = scaled.shape[1]
    norm = jnp.broadcast_to(jnp.sum(scaled * scaled, 0, keepdims=True), (16, count))
    first, second, third = (part.astype(f32) for part in split_three(norm))
    row = lax.broadcasted_iota(jnp.int32, (16, count), 0)
    base = 0 if left else 3
    picked = jnp.where(row == base, first, jnp.where(row == base + 1, second, third))
    inside = (row >= base) & (row < base + 3)
    return jnp.where(inside, picked, jnp.where(row < 6, 1.0, 0.0)).astype(bf16)


def left_rows(scaled):
    a, b, c = split_three(scaled)
    zero = jnp.zeros_like(a)
    return jnp.concatenate([a, a, b, b, a, c, norm_rows(scaled, True), zero], 0)


def right_rows(scaled):
    a, b, c = (-2.0 * part.astype(f32) for part in split_three(scaled))
    a, b, c = a.astype(bf16), b.astype(bf16), c.astype(bf16)
    zero = jnp.zeros_like(a)
    return jnp.concatenate([a, b, a, b, c, a, norm_rows(scaled, False), zero], 0)


def apply_kernel(pieces, *refs):
    gathered, others, scales, out = refs[0], refs[1 : 1 + pieces], refs[1 + pieces], refs[2 + pieces]
    left, right, weights, distance, coarse, fine = refs[3 + pieces :]
    blocks, feat, width = gathered.shape
    probes = out.shape[1]
    scale = scales[:, :1]
    parts = width // tile

    def prepare(block, _):
        place = pl.ds(pl.multiple_of(block * width, width), width)
        left[:, place] = left_rows(gathered[block] * scale)
        return 0

    lax.fori_loop(0, blocks, prepare, 0)
    for index, other in enumerate(others):
        right[index * width : (index + 1) * width, :] = right_rows(other[:feat, :] * scale).T
        probe = other[feat:, :] * probe_factor
        high = probe.astype(bf16)
        low = (probe - high.astype(f32)).astype(bf16)
        weights[index] = jnp.concatenate([high, low], 0)

    tiles = blocks * parts * pieces

    def place_of(number):
        column = number // pieces
        return column, number - column * pieces

    def find_distance(number, slot):
        column, piece = place_of(jnp.minimum(number, tiles - 1))
        rows = right[pl.ds(pl.multiple_of(piece * width, width), width), :]
        columns = left[:, pl.ds(pl.multiple_of(column * tile, tile), tile)]
        distance[slot] = jnp.dot(rows, columns, preferred_element_type=f32)

    def find_value(slot):
        for row in range(0, width, strip):
            here = slice(row, row + strip)
            squared = jnp.maximum(distance[slot, here, :], 1e-30)
            z = -shift - squared * lax.rsqrt(squared)
            value = (z * z + constant) * jnp.exp2(z)
            high = value.astype(bf16)
            coarse[slot, here, :] = high
            fine[slot, here, :] = (value - high.astype(f32)).astype(bf16)

    def add_product(number, slot):
        column, piece = place_of(jnp.maximum(number, 0))
        weight = weights[piece]
        large = jnp.dot(weight, coarse[slot], preferred_element_type=f32)
        small = jnp.dot(weight[:probes], fine[slot], preferred_element_type=f32)
        total = large[:probes] + large[probes:] + small
        block = column // parts
        place = pl.ds(pl.multiple_of((column - block * parts) * tile, tile), tile)
        before = jnp.where(piece == 0, 0.0, out[block, :, place])
        out[block, :, place] = before + total

    for slot in range(2):
        find_distance(slot, slot)

    def step(index, _):
        for slot in range(2):
            number = 2 * index + slot
            add_product(number - 1, 1 - slot)
            find_value(slot)
            find_distance(number + 2, slot)
        return 0

    lax.fori_loop(0, tiles // 2, step, 0)
    add_product(tiles - 1, 1)


def apply_pieces(gathered, others, scales):
    blocks, feat, width = gathered.shape
    pieces = len(others)
    probes = others[0].shape[0] - feat
    values = blocks * width * pieces * width
    return pl.pallas_call(
        functools.partial(apply_kernel, pieces),
        out_shape=jax.ShapeDtypeStruct((blocks, probes, width), f32),
        in_specs=[vmem] * (2 + pieces),
        out_specs=vmem,
        scratch_shapes=[
            pltpu.VMEM((8 * feat, blocks * width), bf16),
            pltpu.VMEM((pieces * width, 8 * feat), bf16),
            pltpu.VMEM((pieces, 2 * probes, width), bf16),
            pltpu.VMEM((2, width, tile), f32),
            pltpu.VMEM((2, width, tile), bf16),
            pltpu.VMEM((2, width, tile), bf16),
        ],
        compiler_params=pltpu.CompilerParams(vmem_limit_bytes=10 * 2**20),
        cost_estimate=pl.CostEstimate(flops=values * 1000, bytes_accessed=values // 8, transcendentals=2 * values),
        name="apply_pieces",
    )(gathered, *others, scales)


def pack_kernel(points, probes, scales, pairing, travel, copies, column, branch, once, pairing_here, scales_here, sems):
    feat = points.shape[0]
    third = pltpu.make_async_copy(pairing, pairing_here, sems.at[2])
    third.start()
    fourth = pltpu.make_async_copy(scales, scales_here, sems.at[3])
    fourth.start()
    first = pltpu.make_async_copy(points, travel.at[:feat], sems.at[0])
    second = pltpu.make_async_copy(probes, travel.at[feat:], sems.at[1])
    first.start()
    second.start()
    third.wait()
    branch[0] = pairing_here[1] - 1
    once[0] = jnp.minimum(pairing_here[1], 1)
    fourth.wait()
    row = lax.broadcasted_iota(jnp.int32, column.shape, 0)
    factors = jnp.zeros(column.shape, f32)
    for index in range(feat):
        factors = jnp.where(row == index, scales_here[index] * feature_factor, factors)
    column[...] = factors
    first.wait()
    second.wait()
    for block in range(copies.shape[0]):
        copies[block] = travel[:feat, :]


def pack(points, probes, scales, pairing, rows):
    return pl.pallas_call(
        pack_kernel,
        out_shape=(
            jax.ShapeDtypeStruct((points.shape[0] + probes.shape[0], points.shape[1]), f32),
            jax.ShapeDtypeStruct((rows, *points.shape), f32),
            jax.ShapeDtypeStruct((points.shape[0], 128), f32),
            jax.ShapeDtypeStruct((1,), jnp.int32),
            jax.ShapeDtypeStruct((1,), jnp.int32),
        ),
        in_specs=[anywhere] * 4,
        out_specs=(vmem, vmem, vmem, smem, smem),
        scratch_shapes=[
            pltpu.SMEM((2,), jnp.int32),
            pltpu.SMEM((points.shape[0],), f32),
            pltpu.SemaphoreType.DMA((4,)),
        ],
        name="pack",
    )(points, probes, scales, pairing)


def swap(value, axis, mask):
    pairs = [(source, source ^ mask) for source in range(lax.axis_size(axis))]
    return lax.ppermute(value, axis, pairs)


def body(points, probes, scales, noise, pairing):
    count = lax.axis_size("blk")
    rows = lax.axis_size("row")
    feat = points.shape[0]
    travel, copies, column, branch, once = pack(points, probes, scales, pairing, rows)

    def exchange(mask, travel, once, copies):
        first = swap(travel, "blk", count - 1)
        direct = mask <= direct_masks
        second = swap(travel, "blk", mask) if direct else swap(first, "blk", mask ^ (count - 1))
        gathered = lax.cond(once[0] > 0, lambda copies: lax.all_to_all(copies, "row", 0, 0), lambda copies: copies, copies)
        return first, second, gathered

    exchanges = [functools.partial(exchange, mask) for mask in range(1, count - 1)]
    first, second, gathered = lax.switch(branch[0], exchanges, travel, once, copies)
    part = apply_pieces(gathered, [travel, first, second], column)
    parts = lax.all_to_all(part, "row", 0, 0)
    return jnp.sum(parts, 0) + noise[0] * probes


def solution(mesh):
    in_specs = (P(None, ("blk", "row")), P(None, ("blk", "row")), P(), P(), P())
    out_specs = P(None, ("blk", "row"))
    return jax.shard_map(body, mesh=mesh, in_specs=in_specs, out_specs=out_specs, check_vma=False)
```

profile of v0, /device:TPU:8, one launch (start us, length us, event | category | flops | bytes accessed | tf_op | source)
XLA Modules:
  0.0 62.3 jit_solution(6519448479256850218)
XLA Ops:
  0.0 1.4 %pack.1 = (f32[32,512]{1,0:T(8,128)S(1)}, f32[8,16,512]{2,1,0:T(8,128)S(1)}, f32[16,128]{1,0:T(8,128)}, s32[1]{0:T(128)}, s32[1]{0:T(128)}) custom-call(f32[16,512]{1,0:T(8,128)} %points.1, f32[16,512]{1,0:T(8,128)} %probes.1, f32[16]{0:T(128)} %scales.1, s32[2]{0:T(128)} %pairing.1), custom_call_target="tpu_custom_call" | custom-call | tf_op jit(solution)/shard_map/pack/pallas_call | solution.py:179
  2.0 0.0 copy-start
  2.1 33.8 %conditional.63 = (f32[32,512]{1,0:T(8,128)}, f32[32,512]{1,0:T(8,128)}, f32[8,16,512]{2,1,0:T(8,128)S(1)}) conditional(s32[]{:T(128)} %bitcast.62, (f32[32,512]{1,0:T(8,128)S(1)}, s32[1]{0:T(128)}, f32[8,16,512]{2,1,0:T(8,128)S(1)}) %tuple.625, (f32[32,512]{1,0:T(8,128)S(1)}, s32[1]{0:T(128)}, ...), branch_computations={%region_0.0_spmd, %region_3.0_spmd, %region_6.0_spmd, %region_9.0_... | conditional | flops 2 | bytes 1572990 | solution.py:218
  2.4 14.0 %collective-permute-start.88 = (f32[32,512]{1,0:T(8,128)S(1)}, f32[32,512]{1,0:T(8,128)}, u32[]{:S(2)}, u32[]{:S(2)}) collective-permute-start(f32[32,512]{1,0:T(8,128)S(1)} %get-tuple-element.819), channel_id=1, source_target_pairs={{0,504},{8,496},{16,488},{24,480},{32,472},{40,464},{48,456},{56,4... | collective-permute-start | bytes 196616 | tf_op jit(solution)/shard_map/cond/branch_44_fun/ppermute | solution.py:201
  16.3 2.7 %collective-permute-done.88 = f32[32,512]{1,0:T(8,128)} collective-permute-done((f32[32,512]{1,0:T(8,128)S(1)}, f32[32,512]{1,0:T(8,128)}, u32[]{:S(2)}, u32[]{:S(2)}) %collective-permute-start.88) | collective-permute-done | bytes 65568 | tf_op jit(solution)/shard_map/cond/branch_44_fun/ppermute | solution.py:201
  19.1 1.9 %collective-permute-start.89 = (f32[32,512]{1,0:T(8,128)}, f32[32,512]{1,0:T(8,128)}, u32[]{:S(2)}, u32[]{:S(2)}) collective-permute-start(f32[32,512]{1,0:T(8,128)} %collective-permute-done.88), channel_id=1, source_target_pairs={{0,144},{8,152},{16,128},{24,136},{32,176},{40,184},{48,160},{56,1... | collective-permute-start | bytes 196616 | tf_op jit(solution)/shard_map/cond/branch_44_fun/ppermute | solution.py:201
  21.7 13.7 %conditional.44 = (f32[8,16,512]{2,1,0:T(8,128)S(1)}) conditional(s32[]{:T(128)} %bitcast.44, f32[8,16,512]{2,1,0:T(8,128)S(1)} %get-tuple-element.821, f32[8,16,512]{2,1,0:T(8,128)S(1)} %get-tuple-element.821), branch_computations={%region_133.0_spmd, %region_134.0_spmd} | conditional | bytes 524296 | solution.py:214
  21.7 13.7 %all_to_all.297 = f32[8,16,512]{2,1,0:T(8,128)S(1)} all-to-all(f32[8,16,512]{2,1,0:T(8,128)S(1)} %param.133), channel_id=1, replica_groups=mesh['blk'=64,'row'=8] {'row'}, dimensions={0} | all-to-all | bytes 524288 | tf_op jit(solution)/shard_map/cond/branch_44_fun/cond/branch_1_fun/all_to_all | solution.py:214
  35.4 0.0 collective-permute-done.89
  35.9 0.0 copy-done
  35.9 14.6 %apply_pieces.1 = f32[8,16,512]{2,1,0:T(8,128)} custom-call(f32[8,16,512]{2,1,0:T(8,128)S(1)} %get-tuple-element.885.refs_0_, f32[32,512]{1,0:T(8,128)S(1)} %get-tuple-element.882.refs_1_, f32[32,512]{1,0:T(8,128)} %get-tuple-element.886.refs_2_, f32[32,512]{1,0:T(8,128)} %get-tuple-element.887.refs_3_, f32[16,128]{1,0:T(8,128)S(1)} %copy-done), custom_call_target="tpu_custom_call" | custom-call | flops 6291456000 | bytes 786432 | tf_op jit(solution)/shard_map/apply_pieces/pallas_call | solution.py:134
  50.5 3.4 %all-to-all-start.62 = ((f32[8,16,512]{2,1,0:T(8,128)}), f32[8,16,512]{2,1,0:T(8,128)S(1)}, u32[]{:S(2)}, u32[]{:S(2)}) async-start(f32[8,16,512]{2,1,0:T(8,128)} %apply_pieces.1), calls=%async_computation.62 | async-start | bytes 524288 | tf_op jit(solution)/shard_map/all_to_all | solution.py:220
  54.6 0.0 copy-start.1
  54.6 7.1 %all-to-all-done.62 = f32[8,16,512]{2,1,0:T(8,128)S(1)} async-done(((f32[8,16,512]{2,1,0:T(8,128)}), f32[8,16,512]{2,1,0:T(8,128)S(1)}, u32[]{:S(2)}, u32[]{:S(2)}) %all-to-all-start.62) | async-done | bytes 262176 | tf_op jit(solution)/shard_map/all_to_all | solution.py:220
  61.7 0.0 copy-done.1
  61.7 0.6 multiply_add_fusion
  (2 shorter events, 0.0 us)
Async XLA Ops:
  2.0 33.8 %copy-start = (f32[16,128]{1,0:T(8,128)S(1)}, f32[16,128]{1,0:T(8,128)}, u32[]{:S(2)}) copy-start(f32[16,128]{1,0:T(8,128)} %get-tuple-element.888.refs_4_) | copy-start | bytes 24580
  2.4 16.7 %collective-permute-start.88 = (f32[32,512]{1,0:T(8,128)S(1)}, f32[32,512]{1,0:T(8,128)}, u32[]{:S(2)}, u32[]{:S(2)}) collective-permute-start(f32[32,512]{1,0:T(8,128)S(1)} %get-tuple-element.819), channel_id=1, source_target_pairs={{0,504},{8,496},{16,488},{24,480},{32,472},{40,464},{48,456},{56,4... | collective-permute-start | bytes 196616 | tf_op jit(solution)/shard_map/cond/branch_44_fun/ppermute | solution.py:201
  19.1 16.3 %collective-permute-start.89 = (f32[32,512]{1,0:T(8,128)}, f32[32,512]{1,0:T(8,128)}, u32[]{:S(2)}, u32[]{:S(2)}) collective-permute-start(f32[32,512]{1,0:T(8,128)} %collective-permute-done.88), channel_id=1, source_target_pairs={{0,144},{8,152},{16,128},{24,136},{32,176},{40,184},{48,160},{56,1... | collective-permute-start | bytes 196616 | tf_op jit(solution)/shard_map/cond/branch_44_fun/ppermute | solution.py:201
  50.5 11.2 %all-to-all-start.62 = ((f32[8,16,512]{2,1,0:T(8,128)}), f32[8,16,512]{2,1,0:T(8,128)S(1)}, u32[]{:S(2)}, u32[]{:S(2)}) async-start(f32[8,16,512]{2,1,0:T(8,128)} %apply_pieces.1), calls=%async_computation.62 | async-start | bytes 524288 | tf_op jit(solution)/shard_map/all_to_all | solution.py:220
  54.6 7.1 %copy-start.1 = (f32[16,512]{1,0:T(8,128)S(1)}, f32[16,512]{1,0:T(8,128)}, u32[]{:S(2)}) copy-start(f32[16,512]{1,0:T(8,128)} %probes.1) | copy-start | bytes 98308
where the time goes:
time: 62.8 us; the launch traced here: 62.3 us
  starting transfers between devices  19.3 us (31%)
  Pallas kernels  16 us (25%)
  blocking collectives  13.7 us (22%)
  waiting for transfers between devices  9.82 us (16%)
  loops' own time  1.53 us (2%)
  between operations  1.33 us (2%)
  other arithmetic  0.64 us (1%)
    ppermute x2, starting transfers between devices, swap(): return lax.ppermute(value, axis, pairs)  15.9 us
    pallas_call x1, Pallas kernels, apply_pieces(): pl.pallas_call(functools.partial(apply_kernel, pieces), out_shape=jax.Sha...  14.6 us
    all_to_all x1, blocking collectives, exchange(): lax.all_to_all(copies, 'row', 0, 0)  13.7 us
    all_to_all x1, waiting for transfers between devices, body(): parts = lax.all_to_all(part, 'row', 0, 0)  7.08 us
    all_to_all x1, starting transfers between devices, body(): parts = lax.all_to_all(part, 'row', 0, 0)  3.41 us
    ppermute x2, waiting for transfers between devices, swap(): return lax.ppermute(value, axis, pairs)  2.73 us
    another operation x1, loops' own time, body(): lax.switch(branch[0], exchanges, travel, once, copies)  1.51 us
    pallas_call x1, Pallas kernels, pack(): pl.pallas_call(pack_kernel, out_shape=(jax.ShapeDtypeStruct((points.shape...  1.42 us
  transfers between devices with their start and end apart: 3, of which 2 were waited for; matrix products, arithmetic and copies ran while one was open for 0% of the time, Pallas kernels for 0%

commit v1 on v0

--- a/solution.py
+++ b/solution.py
@@ -70,7 +70,7 @@
         left[:, place] = left_rows(gathered[block] * scale)
         return 0
 
-    lax.fori_loop(0, blocks, prepare, 0)
+    lax.fori_loop(0, blocks, prepare, 0, unroll=4)
     for index, other in enumerate(others):
         right[index * width : (index + 1) * width, :] = right_rows(other[:feat, :] * scale).T
         probe = other[feat:, :] * probe_factor

time: 62.8 us -> 67.2 us (1.070)
  the two profiles are of different devices: /device:TPU:8 before, /device:TPU:16 now
where the time goes in v1:
time: 67.2 us; the launch traced here: 66.8 us
  starting transfers between devices  21.3 us (32%)
  Pallas kernels  15.6 us (23%)
  blocking collectives  12.8 us (19%)
  waiting for transfers between devices  9.38 us (14%)
  loops' own time  5.76 us (9%)
  between operations  1.33 us (2%)
    ppermute x2, starting transfers between devices, swap(): return lax.ppermute(value, axis, pairs)  17.8 us
    pallas_call x1, Pallas kernels, apply_pieces(): pl.pallas_call(functools.partial(apply_kernel, pieces), out_shape=jax.Sha...  14.2 us
    all_to_all x1, blocking collectives, exchange(): lax.all_to_all(copies, 'row', 0, 0)  12.8 us
    all_to_all x1, waiting for transfers between devices, body(): parts = lax.all_to_all(part, 'row', 0, 0)  6.56 us
    another operation x1, loops' own time, body(): lax.switch(branch[0], exchanges, travel, once, copies)  5.75 us
    all_to_all x1, starting transfers between devices, body(): parts = lax.all_to_all(part, 'row', 0, 0)  3.41 us
    ppermute x2, waiting for transfers between devices, swap(): return lax.ppermute(value, axis, pairs)  2.82 us
    pallas_call x1, Pallas kernels, pack(): pl.pallas_call(pack_kernel, out_shape=(jax.ShapeDtypeStruct((points.shape...  1.42 us
  transfers between devices with their start and end apart: 3, of which 2 were waited for; matrix products, arithmetic and copies ran while one was open for 0% of the time, Pallas kernels for 0%

profile of v1, /device:TPU:16, one launch (start us, length us, event | category | flops | bytes accessed | tf_op | source)
XLA Modules:
  0.0 66.8 jit_solution(6166949171843703224)
XLA Ops:
  0.0 1.4 %pack.1 = (f32[32,512]{1,0:T(8,128)S(1)}, f32[8,16,512]{2,1,0:T(8,128)S(1)}, f32[16,128]{1,0:T(8,128)}, s32[1]{0:T(128)}, s32[1]{0:T(128)}) custom-call(f32[16,512]{1,0:T(8,128)} %points.1, f32[16,512]{1,0:T(8,128)} %probes.1, f32[16]{0:T(128)} %scales.1, s32[2]{0:T(128)} %pairing.1), custom_call_target="tpu_custom_call" | custom-call | tf_op jit(solution)/shard_map/pack/pallas_call | solution.py:179
  2.0 0.0 copy-start
  2.1 39.3 %conditional.63 = (f32[32,512]{1,0:T(8,128)}, f32[32,512]{1,0:T(8,128)}, f32[8,16,512]{2,1,0:T(8,128)S(1)}) conditional(s32[]{:T(128)} %bitcast.62, (f32[32,512]{1,0:T(8,128)S(1)}, s32[1]{0:T(128)}, f32[8,16,512]{2,1,0:T(8,128)S(1)}) %tuple.625, (f32[32,512]{1,0:T(8,128)S(1)}, s32[1]{0:T(128)}, ...), branch_computations={%region_0.0_spmd, %region_3.0_spmd, %region_6.0_spmd, %region_9.0_... | conditional | flops 2 | bytes 1572990 | solution.py:218
  6.9 13.7 %collective-permute-start.98 = (f32[32,512]{1,0:T(8,128)S(1)}, f32[32,512]{1,0:T(8,128)}, u32[]{:S(2)}, u32[]{:S(2)}) collective-permute-start(f32[32,512]{1,0:T(8,128)S(1)} %get-tuple-element.834), channel_id=1, source_target_pairs={{0,504},{8,496},{16,488},{24,480},{32,472},{40,464},{48,456},{56,4... | collective-permute-start | bytes 196616 | tf_op jit(solution)/shard_map/cond/branch_49_fun/ppermute | solution.py:201
  20.6 2.8 %collective-permute-done.98 = f32[32,512]{1,0:T(8,128)} collective-permute-done((f32[32,512]{1,0:T(8,128)S(1)}, f32[32,512]{1,0:T(8,128)}, u32[]{:S(2)}, u32[]{:S(2)}) %collective-permute-start.98) | collective-permute-done | bytes 65568 | tf_op jit(solution)/shard_map/cond/branch_49_fun/ppermute | solution.py:201
  23.4 4.1 %collective-permute-start.99 = (f32[32,512]{1,0:T(8,128)}, f32[32,512]{1,0:T(8,128)}, u32[]{:S(2)}, u32[]{:S(2)}) collective-permute-start(f32[32,512]{1,0:T(8,128)} %collective-permute-done.98), channel_id=1, source_target_pairs={{0,104},{8,96},{16,120},{24,112},{32,72},{40,64},{48,88},{56,80},{... | collective-permute-start | bytes 196616 | tf_op jit(solution)/shard_map/cond/branch_49_fun/ppermute | solution.py:201
  28.2 12.8 %conditional.49 = (f32[8,16,512]{2,1,0:T(8,128)S(1)}) conditional(s32[]{:T(128)} %bitcast.49, f32[8,16,512]{2,1,0:T(8,128)S(1)} %get-tuple-element.836, f32[8,16,512]{2,1,0:T(8,128)S(1)} %get-tuple-element.836), branch_computations={%region_148.0_spmd, %region_149.0_spmd} | conditional | bytes 524296 | solution.py:214
  28.3 12.8 %all_to_all.302 = f32[8,16,512]{2,1,0:T(8,128)S(1)} all-to-all(f32[8,16,512]{2,1,0:T(8,128)S(1)} %param.148), channel_id=1, replica_groups=mesh['blk'=64,'row'=8] {'row'}, dimensions={0} | all-to-all | bytes 524288 | tf_op jit(solution)/shard_map/cond/branch_49_fun/cond/branch_1_fun/all_to_all | solution.py:214
  41.1 0.0 collective-permute-done.99
  41.3 0.0 copy-done
  41.3 14.2 %apply_pieces.1 = f32[8,16,512]{2,1,0:T(8,128)} custom-call(f32[8,16,512]{2,1,0:T(8,128)S(1)} %get-tuple-element.885.refs_0_, f32[32,512]{1,0:T(8,128)S(1)} %get-tuple-element.882.refs_1_, f32[32,512]{1,0:T(8,128)} %get-tuple-element.886.refs_2_, f32[32,512]{1,0:T(8,128)} %get-tuple-element.887.refs_3_, f32[16,128]{1,0:T(8,128)S(1)} %copy-done), custom_call_target="tpu_custom_call" | custom-call | flops 6291456000 | bytes 786432 | tf_op jit(solution)/shard_map/apply_pieces/pallas_call | solution.py:134
  55.5 3.4 %all-to-all-start.62 = ((f32[8,16,512]{2,1,0:T(8,128)}), f32[8,16,512]{2,1,0:T(8,128)S(1)}, u32[]{:S(2)}, u32[]{:S(2)}) async-start(f32[8,16,512]{2,1,0:T(8,128)} %apply_pieces.1), calls=%async_computation.62 | async-start | bytes 524288 | tf_op jit(solution)/shard_map/all_to_all | solution.py:220
  59.6 0.0 copy-start.1
  59.6 6.6 %all-to-all-done.62 = f32[8,16,512]{2,1,0:T(8,128)S(1)} async-done(((f32[8,16,512]{2,1,0:T(8,128)}), f32[8,16,512]{2,1,0:T(8,128)S(1)}, u32[]{:S(2)}, u32[]{:S(2)}) %all-to-all-start.62) | async-done | bytes 262176 | tf_op jit(solution)/shard_map/all_to_all | solution.py:220
  66.2 0.0 copy-done.1
  66.2 0.6 multiply_add_fusion
  (2 shorter events, 0.0 us)
Async XLA Ops:
  2.0 39.3 %copy-start = (f32[16,128]{1,0:T(8,128)S(1)}, f32[16,128]{1,0:T(8,128)}, u32[]{:S(2)}) copy-start(f32[16,128]{1,0:T(8,128)} %get-tuple-element.888.refs_4_) | copy-start | bytes 24580
  6.9 16.6 %collective-permute-start.98 = (f32[32,512]{1,0:T(8,128)S(1)}, f32[32,512]{1,0:T(8,128)}, u32[]{:S(2)}, u32[]{:S(2)}) collective-permute-start(f32[32,512]{1,0:T(8,128)S(1)} %get-tuple-element.834), channel_id=1, source_target_pairs={{0,504},{8,496},{16,488},{24,480},{32,472},{40,464},{48,456},{56,4... | collective-permute-start | bytes 196616 | tf_op jit(solution)/shard_map/cond/branch_49_fun/ppermute | solution.py:201
  23.4 17.7 %collective-permute-start.99 = (f32[32,512]{1,0:T(8,128)}, f32[32,512]{1,0:T(8,128)}, u32[]{:S(2)}, u32[]{:S(2)}) collective-permute-start(f32[32,512]{1,0:T(8,128)} %collective-permute-done.98), channel_id=1, source_target_pairs={{0,104},{8,96},{16,120},{24,112},{32,72},{40,64},{48,88},{56,80},{... | collective-permute-start | bytes 196616 | tf_op jit(solution)/shard_map/cond/branch_49_fun/ppermute | solution.py:201
  55.5 10.6 %all-to-all-start.62 = ((f32[8,16,512]{2,1,0:T(8,128)}), f32[8,16,512]{2,1,0:T(8,128)S(1)}, u32[]{:S(2)}, u32[]{:S(2)}) async-start(f32[8,16,512]{2,1,0:T(8,128)} %apply_pieces.1), calls=%async_computation.62 | async-start | bytes 524288 | tf_op jit(solution)/shard_map/all_to_all | solution.py:220
  59.6 6.6 %copy-start.1 = (f32[16,512]{1,0:T(8,128)S(1)}, f32[16,512]{1,0:T(8,128)}, u32[]{:S(2)}) copy-start(f32[16,512]{1,0:T(8,128)} %probes.1) | copy-start | bytes 98308
